TPU v7x, 256 devices: a whole 4x4x8 slice. The times are simulated.
256 devices in a mesh: dp: 8 (over z_hi, core), seq: 32 (over x, y, z_lo).
Axes of the slice: x: 4, y: 4, z: 8 (z_hi: 4, z_lo: 2; z = z_hi * 2 + z_lo), core: 2. Of those that a mesh axis runs over, the one named last changes fastest.
Arguments:
- queries: bfloat16 [8, 8192, 1024], P('dp', 'seq'), may hold values from -6 to 6
- image_feats: bfloat16 [8, 32, 64, 8192], P('dp', 'seq'), may hold values from -6 to 6
- key_weight: bfloat16 [8192, 128], replicated, may hold values from -0.0625 to 0.0625
- value_weight: bfloat16 [8192, 128], replicated, may hold values from -0.0625 to 0.0625
- image_pos: int32 [8, 32], P('dp'), may hold values from 0 to 8191, as said below
- image_slot: int32 [8, 32], P('dp'), may hold values from 0 to 31, each once within a row
- ctx_grad: bfloat16 [8, 8192, 1024], P('dp', 'seq'), may hold values from -24 to 24
Outputs:
- context: bfloat16 [8, 8192, 1024], P('dp', 'seq')
- query_grad: bfloat16 [8, 8192, 1024], P('dp', 'seq')
- feats_grad: bfloat16 [8, 32, 64, 8192], P('dp', 'seq')
- key_wgrad: float32 [8192, 128], P('seq')
- value_wgrad: float32 [8192, 128], P('seq')
Inputs may be any that keep to these rules, and one draw needn't show every extreme that they name: `image_pos`: for each document the positions rise strictly, the first is 0 and the last is 8191. Each document's row is a permutation: image i is stored in slot image_slot[i], held by seq index image_slot[i].
All inputs are finite; a program needn't handle non-finite values.
Results may differ from a plain program's by a relative error of at most 0.0075.
Values may be sent and summed in bfloat16 or wider, within the bound.
A program may use at most 128 MiB of HBM per device.

v0:
```python
import jax
import jax.numpy as jnp
from jax import lax
from jax.sharding import PartitionSpec as P

NORM_EPS = 1e-05


def norm_rows(inputs):
    return inputs * lax.rsqrt(jnp.mean(inputs * inputs, axis=-1, keepdims=True) + NORM_EPS)


def norm_back(inputs, upstream):
    factor = lax.rsqrt(jnp.mean(inputs * inputs, axis=-1, keepdims=True) + NORM_EPS)
    normed = inputs * factor
    return factor * (upstream - normed * jnp.mean(upstream * normed, axis=-1, keepdims=True))


def slot_positions(image_pos, image_slot):
    image_count = image_slot.shape[0]
    matches = image_slot[:, None] == jnp.arange(image_count, dtype=jnp.int32)[None, :]
    return jnp.sum(jnp.where(matches, image_pos[:, None], 0), axis=0)


def attend_block(query_block, ctx_block, tok_pos, key_table, value_table, key_pos, score_scale):
    across = (((1,), (1,)), ((), ()))
    stacked = (((0,), (0,)), ((), ()))
    scores = (
        lax.dot_general(query_block, key_table, across, preferred_element_type=jnp.float32)
        * score_scale
    )
    visible = key_pos[None, :] <= tok_pos[:, None]
    exp_scores = jnp.where(visible, jnp.exp(scores), jnp.zeros_like(scores))
    soft_weights = exp_scores / jnp.sum(exp_scores, axis=1, keepdims=True)
    soft_round = soft_weights.astype(jnp.bfloat16)
    context = jnp.dot(soft_round, value_table, preferred_element_type=jnp.float32).astype(
        jnp.bfloat16
    )
    prob_grad = lax.dot_general(ctx_block, value_table, across, preferred_element_type=jnp.float32)
    centre = jnp.sum(soft_weights * prob_grad, axis=1, keepdims=True)
    score_full = soft_weights * (prob_grad - centre) * score_scale
    score_grad = score_full.astype(jnp.bfloat16)
    query_grad = jnp.dot(score_grad, key_table, preferred_element_type=jnp.float32)
    key_part = lax.dot_general(
        score_full,
        query_block.astype(jnp.float32),
        stacked,
        precision=lax.Precision.HIGHEST,
        preferred_element_type=jnp.float32,
    )
    value_part = lax.dot_general(soft_round, ctx_block, stacked, preferred_element_type=jnp.float32)
    return (context, query_grad, key_part, value_part)


def attend_all(normed, ctx_rows, tok_pos, key_table, value_table, key_pos, block_rows):
    total_rows, head_dim = normed.shape
    block_count = total_rows // block_rows
    score_scale = head_dim ** (-0.5)

    def scan_step(running, block_item):
        results = attend_block(
            block_item[0],
            block_item[1],
            block_item[2],
            key_table,
            value_table,
            key_pos,
            score_scale,
        )
        return ((running[0] + results[2], running[1] + results[3]), (results[0], results[1]))

    zero_grad = jnp.zeros((key_table.shape[0], head_dim), jnp.float32)
    block_items = (
        normed.reshape(block_count, block_rows, head_dim),
        ctx_rows.reshape(block_count, block_rows, head_dim),
        tok_pos.reshape(block_count, block_rows),
    )
    grad_sums, outputs = lax.scan(scan_step, (zero_grad, zero_grad), block_items)
    context = outputs[0].reshape(total_rows, head_dim)
    query_grad = outputs[1].reshape(total_rows, head_dim)
    return (context, query_grad, grad_sums[0], grad_sums[1])


def local(queries, image_feats, key_weight, value_weight, image_pos, image_slot, ctx_grad):
    model_width, head_dim = key_weight.shape
    tokens = queries.shape[1]
    group_size = queries.shape[2] // head_dim
    seq_count = lax.axis_size("seq")
    seq_rank = lax.axis_index("seq")
    feats = image_feats[0]
    held_images, vision_rows = (feats.shape[0], feats.shape[1])
    images = held_images * seq_count
    feat_rows = feats.reshape(held_images * vision_rows, model_width)
    key_rows = jnp.dot(feat_rows, key_weight, preferred_element_type=jnp.float32)
    norm_keys = norm_rows(key_rows).astype(jnp.bfloat16)
    value_rows = jnp.dot(feat_rows, value_weight, preferred_element_type=jnp.float32).astype(
        jnp.bfloat16
    )
    packed = jnp.concatenate([norm_keys, value_rows], axis=1).reshape(
        held_images, vision_rows, 2 * head_dim
    )
    gathered = lax.all_gather(packed, "seq", axis=0, tiled=True)
    query_raw = queries[0].reshape(tokens, group_size, head_dim).astype(jnp.float32)
    normed = norm_rows(query_raw).astype(jnp.bfloat16).reshape(tokens * group_size, head_dim)
    ctx_rows = ctx_grad[0].reshape(tokens * group_size, head_dim)
    tok_pos = seq_rank * tokens + jnp.arange(tokens * group_size, dtype=jnp.int32) // group_size
    block_rows = min(tokens, max(1, 512 // group_size)) * group_size
    positions = image_pos[0]
    slot_table = image_slot[0]
    key_pos = jnp.repeat(slot_positions(positions, slot_table), vision_rows)
    table_rows = gathered.reshape(images * vision_rows, 2 * head_dim)
    context, normed_grad, key_grad, value_grad = attend_all(
        normed,
        ctx_rows,
        tok_pos,
        table_rows[:, :head_dim],
        table_rows[:, head_dim:],
        key_pos,
        block_rows,
    )
    partial_value = jnp.concatenate(
        [
            key_grad.reshape(images, vision_rows, head_dim),
            value_grad.reshape(images, vision_rows, head_dim),
        ],
        axis=2,
    )
    owned = lax.psum_scatter(partial_value, "seq", scatter_dimension=0, tiled=True).reshape(
        held_images * vision_rows, 2 * head_dim
    )
    key_row_grad = norm_back(key_rows, owned[:, :head_dim]).astype(jnp.bfloat16)
    value_round = owned[:, head_dim:].astype(jnp.bfloat16)
    row_grads = jnp.concatenate([key_row_grad, value_round], axis=1)
    across = (((1,), (1,)), ((), ()))
    stacked = (((0,), (0,)), ((), ()))
    feats_grad = lax.dot_general(
        key_row_grad, key_weight, across, preferred_element_type=jnp.float32
    ) + lax.dot_general(value_round, value_weight, across, preferred_element_type=jnp.float32)
    feats_grad = feats_grad.astype(jnp.bfloat16).reshape(1, held_images, vision_rows, model_width)
    wgrad_piece = lax.psum_scatter(
        lax.dot_general(feat_rows, row_grads, stacked, preferred_element_type=jnp.float32),
        "seq",
        scatter_dimension=0,
        tiled=True,
    )
    wgrad_total = lax.psum(wgrad_piece, "dp")
    query_grad = norm_back(query_raw, normed_grad.reshape(tokens, group_size, head_dim)).astype(
        jnp.bfloat16
    )
    context = context.reshape(1, tokens, group_size * head_dim)
    query_grad = query_grad.reshape(1, tokens, group_size * head_dim)
    return (context, query_grad, feats_grad, wgrad_total[:, :head_dim], wgrad_total[:, head_dim:])


def solution(mesh):
    return jax.shard_map(
        local,
        mesh=mesh,
        in_specs=(
            P("dp", "seq", None),
            P("dp", "seq", None, None),
            P(),
            P(),
            P("dp", None),
            P("dp", None),
            P("dp", "seq", None),
        ),
        out_specs=(
            P("dp", "seq", None),
            P("dp", "seq", None),
            P("dp", "seq", None, None),
            P("seq", None),
            P("seq", None),
        ),
        check_vma=False,
    )
```

profile of v0, /device:TPU:1, one launch (start us, length us, event | category | flops | bytes accessed | tf_op | source)
XLA Modules:
  0.0 709.3 jit_solution(7757932978434025274)
XLA Ops:
  10.6 2.4 convolution_convert_fusion.1
  19.6 2.1 reshape_reshape_squeeze.3
  23.0 127.5 %all-gather.3.cloned.1.call-done = bf16[2048,256]{1,0:T(8,128)(2,1)} async-done(((bf16[64,256]{1,0:T(8,128)(2,1)}), bf16[2048,256]{1,0:T(8,128)(2,1)}) %all-gather.3.cloned.1.call-update) | async-done | bytes 1048592 | tf_op jit(solution)/shard_map/all_gather | solution.py:102
  150.5 2.3 fusion.44
  152.7 81.0 %while.17 = (s32[]{:T(128)}, f32[2048,128]{1,0:T(8,128)}, f32[2048,128]{1,0:T(8,128)}, bf16[4,512,128]{2,1,0:T(8,128)(2,1)}, f32[4,512,128]{2,1,0:T(8,128)}, /*i...) while((s32[]{:T(128)}, f32[2048,128]{1,0:T(8,128)}, ...), condition=%wide.region_6.7_spmd.clone, body=%wide.region_3.6_spmd.clone.sunk | while | flops 2974874624 | bytes 126807560 | solution.py:78
  152.9 2.3 fusion.78
  155.2 2.0 multiply_reduce_fusion.5
  160.7 4.2 convolution_add_fusion.6
  166.1 5.2 convolution_add_fusion.5
  172.9 2.3 fusion.78
  175.2 2.0 multiply_reduce_fusion.5
  180.7 4.5 convolution_add_fusion.6
  186.5 5.2 convolution_add_fusion.5
  193.2 2.3 fusion.78
  201.0 4.5 convolution_add_fusion.6
  206.8 5.2 convolution_add_fusion.5
  213.5 2.3 fusion.78
  215.8 2.0 multiply_reduce_fusion.5
  221.4 4.5 convolution_add_fusion.6
  227.1 5.2 convolution_add_fusion.5
  233.7 3.1 pad_maximum_fusion
  237.1 165.9 %reduce-scatter.3.cloned.1.call-done = f32[1,64,256]{2,1,0:T(8,128)} async-done(((f32[32,64,256]{2,1,0:T(8,128)}), f32[1,64,256]{2,1,0:T(8,128)}) %reduce-scatter.3.cloned.1.call-update) | async-done | bytes 65552 | tf_op jit(solution)/shard_map/reduce_scatter | solution.py:128
  405.6 4.5 convolution_bitcast_fusion
  411.5 2.3 mul.111
  413.8 2.4 reshape_reshape.8
  419.5 2.4 mul.115
  421.9 2.1 reshape_reshape.7
  424.0 3.1 multiply_convert_fusion
  427.0 2.2 fusion.47
  429.2 183.2 %reduce-scatter.5.cloned.1.call-done = f32[256,256]{0,1:T(8,128)} async-done(((f32[8192,256]{0,1:T(8,128)}), f32[256,256]{0,1:T(8,128)}) %reduce-scatter.5.cloned.1.call-update) | async-done | bytes 262160 | tf_op jit(solution)/shard_map/reduce_scatter | solution.py:140
  612.5 4.0 fusion.30
  616.5 83.7 %all-reduce.2.cloned.1.call-done = f32[256,256]{0,1:T(8,128)} async-done(((f32[256,256]{0,1:T(8,128)}), f32[256,256]{0,1:T(8,128)}) %all-reduce.2.cloned.1.call-update) | async-done | bytes 262160 | tf_op jit(solution)/shard_map/psum | solution.py:146
  (146 shorter events, 48.5 us)
Async XLA Ops:
  7.2 143.3 %all-gather.3.cloned.1.call-start = ((), (), s32[]{:S(2)}) async-start(), calls=%async_computation.5 | async-start | bytes 1081344 | tf_op jit(solution)/shard_map/all_gather | solution.py:102
  13.0 8.7 %copy-start.11 = (s32[1,32]{1,0:T(1,128)S(1)}, s32[1,32]{1,0:T(1,128)}, u32[]{:S(2)}) copy-start(s32[1,32]{1,0:T(1,128)} %param.13) | copy-start | bytes 388
  13.0 8.7 %copy-start.12 = (s32[1,32]{1,0:T(1,128)S(1)}, s32[1,32]{1,0:T(1,128)}, u32[]{:S(2)}) copy-start(s32[1,32]{1,0:T(1,128)} %param.14) | copy-start | bytes 388
  13.8 389.2 %reduce-scatter.3.cloned.1.call-start = ((), (), s32[]{:S(2)}) async-start(), calls=%async_computation.2 | async-start | bytes 2162688 | tf_op jit(solution)/shard_map/reduce_scatter | solution.py:128
  15.1 137.6 %copy-start.2 = (f32[4,512,128]{2,1,0:T(8,128)}, f32[4,512,128]{2,1,0:T(8,128)S(1)}, u32[]{:S(2)}) copy-start(f32[4,512,128]{2,1,0:T(8,128)S(1)} %reshape.106) | copy-start | bytes 3145732
  155.2 3.9 copy-start.9
  160.7 4.2 copy-start.5
  160.7 4.2 copy-start.14
  160.7 5.4 copy-start.16
  166.1 5.2 copy-start.8
  172.7 2.4 copy-start.7
  175.2 3.9 copy-start.9
  180.7 4.5 copy-start.5
  180.7 4.5 copy-start.14
  180.7 5.8 copy-start.16
  186.5 5.2 copy-start.8
  195.5 3.9 copy-start.9
  201.0 4.5 copy-start.5
  201.0 4.5 copy-start.14
  201.0 5.8 copy-start.16
  206.8 5.2 copy-start.8
  215.8 3.9 copy-start.9
  221.4 4.5 copy-start.5
  221.4 4.5 copy-start.14
  221.4 5.8 copy-start.16
  227.1 5.2 copy-start.8
  233.7 171.8 %copy-start.1 = (bf16[1,1,64,8192]{3,2,1,0:T(8,128)(2,1)S(1)}, bf16[1,1,64,8192]{3,2,1,0:T(8,128)(2,1)}, u32[]{:S(2)}) copy-start(bf16[1,1,64,8192]{3,2,1,0:T(8,128)(2,1)} %param.10) | copy-start | bytes 3145732
  236.9 375.5 %reduce-scatter.5.cloned.1.call-start = ((), (), s32[]{:S(2)}) async-start(), calls=%async_computation.3 | async-start | bytes 8650752 | tf_op jit(solution)/shard_map/reduce_scatter | solution.py:140
  410.1 6.1 copy-start.3
  410.1 290.1 %all-reduce.2.cloned.1.call-start = ((), (), s32[]{:S(2)}) async-start(), calls=%async_computation.4 | async-start | bytes 524288 | tf_op jit(solution)/shard_map/psum | solution.py:146
  418.0 5.9 copy-start.4
  424.0 188.5 %copy-start.10 = (f32[1,64,256]{2,1,0:T(8,128)S(1)}, f32[1,64,256]{2,1,0:T(8,128)}, u32[]{:S(2)}) copy-start(f32[1,64,256]{2,1,0:T(8,128)} %reduce-scatter.3.cloned.1.call-done) | copy-start | bytes 196612
  (16 other events, 30.4 us)
Sparse Core Ops, SparseCore 0:
  13.9 136.5 all-gather.2
  237.0 165.9 reduce-scatter.2
  410.2 202.1 reduce-scatter.4
  615.1 85.1 all-reduce.1
where the time goes:
time: 711 us; the launch traced here: 709 us
  waiting for transfers between devices  560 us (79%)
  matrix products  82.4 us (12%)
  local copies, waits for them, and re-layouts  37 us (5%)
  other arithmetic  14.9 us (2%)
  between operations  14 us (2%)
    reduce_scatter x1, waiting for transfers between devices, local(): lax.psum_scatter(lax.dot_general(feat_rows, row_grads, stacked, preferred...  183 us
    reduce_scatter x1, waiting for transfers between devices, local(): lax.psum_scatter(partial_value, 'seq', scatter_dimension=0, tiled=True)  166 us
    all_gather x1, waiting for transfers between devices, local(): gathered = lax.all_gather(packed, 'seq', axis=0, tiled=True)  127 us
    psum x1, waiting for transfers between devices, local(): wgrad_total = lax.psum(wgrad_piece, 'dp')  83.7 us
    dot_general x4, matrix products, attend_block(): lax.dot_general(score_full, query_block.astype(jnp.float32), stacked, pre...  20.6 us
    dot_general x4, matrix products, attend_block(): lax.dot_general(soft_round, ctx_block, stacked, preferred_element_type=jn...  17.8 us
  transfers between devices with their start and end apart: 4, of which 4 were waited for; matrix products, arithmetic and copies ran while one was open for 5% of the time, Pallas kernels for 0%

commit v1 on v0

v1 whole, which is shorter than its diff:
```python
import functools

import jax
import jax.numpy as jnp
from jax import lax
from jax.experimental import pallas as pl
from jax.experimental.pallas import tpu as pltpu
from jax.sharding import PartitionSpec as P

NORM_EPS = 1e-05
LOG2E = 1.4426950408889634
HIDE = -30000.0
GROUP_DEVICES = 4
BF16 = jnp.bfloat16
F32 = jnp.float32
MESH = pl.DeviceIdType.MESH
ACROSS = (((1,), (1,)), ((), ()))


def dot(a, b):
    return jnp.dot(a, b, preferred_element_type=F32)


def dot_across(a, b):
    return lax.dot_general(a, b, ACROSS, preferred_element_type=F32)


def row_factor(rows):
    return lax.rsqrt(jnp.mean(rows * rows, axis=-1, keepdims=True) + NORM_EPS)


def norm_back(rows, upstream):
    factor = row_factor(rows)
    normed = rows * factor
    return factor * (upstream - normed * jnp.mean(upstream * normed, axis=-1, keepdims=True))


def kernel(
    ns,
    nd,
    q_hbm,
    f_hbm,
    wk_hbm,
    wv_hbm,
    pos_ref,
    slot_ref,
    c_hbm,
    ctx_hbm,
    qg_hbm,
    fg_hbm,
    kw_hbm,
    vw_hbm,
    q_s,
    c_s,
    f_s,
    w_s,
    key_s,
    kv_s,
    y_s,
    do_s,
    vt_s,
    kt_s,
    e_s,
    ot_s,
    ctx_s,
    qg_s,
    fg_s,
    fsl_s,
    sendv_s,
    sendk_s,
    rsv_s,
    rsk_s,
    gv_s,
    gk_s,
    dp1_s,
    dp1r_s,
    dp2_s,
    in_sem,
    out_sem,
    ag_send,
    ag_recv,
    xs,
    xr,
):
    tokens, width = q_s.shape
    hd = 128
    heads = width // hd
    vt, d = f_s.shape
    ds_cols = d // ns
    chunk = GROUP_DEVICES * vt
    ng = ns // GROUP_DEVICES
    keys = ns * vt
    scale = hd ** (-0.5)
    dp_rows = ds_cols // nd

    me = lax.axis_index("seq")
    doc = lax.axis_index("dp")
    my_group = lax.div(me, GROUP_DEVICES)
    my_place = lax.rem(me, GROUP_DEVICES)

    def peer(g, j):
        return lax.rem(my_group + g, ng) * GROUP_DEVICES + lax.rem(my_place + j, GROUP_DEVICES)

    def doc_peer(o):
        return lax.rem(doc + o, nd)

    def block(index, size):
        return pl.ds(pl.multiple_of(index * size, size), size)

    pairs = [(g, j) for g in range(ng) for j in range(GROUP_DEVICES) if (g, j) != (0, 0)]

    steps = 4
    depth = d // steps
    w_copies = []
    for k in range(steps):
        rows = pl.ds(k * depth, depth)
        w_copies.append(
            (
                pltpu.make_async_copy(f_hbm.at[:, rows], f_s.at[:, rows], in_sem.at[3 * k]),
                pltpu.make_async_copy(
                    wk_hbm.at[rows, :], w_s.at[rows, pl.ds(0, hd)], in_sem.at[3 * k + 1]
                ),
                pltpu.make_async_copy(
                    wv_hbm.at[rows, :], w_s.at[rows, pl.ds(hd, hd)], in_sem.at[3 * k + 2]
                ),
            )
        )
    q_copy = pltpu.make_async_copy(q_hbm, q_s, in_sem.at[3 * steps])
    c_copy = pltpu.make_async_copy(c_hbm, c_s, in_sem.at[3 * steps + 1])
    for copies in w_copies:
        for copy in copies:
            copy.start()
    q_copy.start()
    c_copy.start()

    barrier = pltpu.get_barrier_semaphore()
    for g, j in pairs:
        pl.semaphore_signal(barrier, inc=1, device_id={"seq": peer(g, j)}, device_id_type=MESH)
    for o in range(1, nd):
        pl.semaphore_signal(barrier, inc=1, device_id={"dp": doc_peer(o)}, device_id_type=MESH)

    rows_kv = jnp.zeros((vt, 2 * hd), F32)
    for k in range(steps):
        for copy in w_copies[k]:
            copy.wait()
        rows = pl.ds(k * depth, depth)
        rows_kv = rows_kv + dot(f_s[:, rows], w_s[rows, :])
    key_rows = rows_kv[:, :hd]
    key_s[...] = key_rows
    mine = block(me, vt)
    kv_s[mine, :] = jnp.concatenate(
        [(key_rows * row_factor(key_rows)).astype(BF16), rows_kv[:, hd:].astype(BF16)], axis=1
    )
    pl.semaphore_wait(barrier, ns - 1 + nd - 1)

    def send(src, dst, send_sem, recv_sem, target):
        pltpu.make_async_remote_copy(
            src_ref=src,
            dst_ref=dst,
            send_sem=send_sem,
            recv_sem=recv_sem,
            device_id=target,
            device_id_type=MESH,
        ).start()

    def take(ref, sem):
        pltpu.make_async_copy(ref, ref, sem).wait()

    for g, j in pairs:
        send(kv_s.at[mine, :], kv_s.at[mine, :], ag_send.at[0], ag_recv.at[g], {"seq": peer(g, j)})

    lane = lax.broadcasted_iota(jnp.int32, (tokens, hd), 1)
    tok = me * tokens + lax.broadcasted_iota(jnp.int32, (tokens, hd), 0)
    hidden = jnp.where(pos_ref[...] > tok, HIDE, 0.0).astype(BF16)
    q_copy.wait()
    for h in range(heads):
        raw = q_s[:, pl.ds(h * hd, hd)].astype(F32)
        rows = pl.ds(h * tokens, tokens)
        y_s[rows, pl.ds(0, hd)] = (raw * row_factor(raw)).astype(BF16)
        y_s[rows, pl.ds(hd, hd)] = hidden

    def first_pass(g, first):
        group = lax.rem(my_group - g + ng, ng)
        rows = block(group, chunk)
        pair = kv_s[rows, :]
        slot_of_key = group * GROUP_DEVICES + lax.div(
            lax.broadcasted_iota(jnp.int32, (chunk, hd), 0), vt
        )
        marks = (slot_ref[...] == slot_of_key).astype(F32).astype(BF16)
        key_aug = jnp.concatenate([pair[:, :hd], marks], axis=1)
        value_t = pair[:, hd:].astype(F32).T.astype(BF16)
        kt_s[:, rows] = pair[:, :hd].astype(F32).T.astype(BF16)
        value_aug = jnp.concatenate([value_t, jnp.ones((hd, chunk), BF16)], axis=0)
        for h in range(heads):
            head = pl.ds(h * tokens, tokens)
            scores = dot_across(key_aug, y_s[head, :])
            weights = jnp.exp2(scores * (scale * LOG2E)).astype(BF16)
            e_s[rows, head] = weights
            part = dot(value_aug, weights)
            if first:
                ot_s[h] = part
            else:
                ot_s[h] += part

    take(kv_s.at[pl.ds(0, chunk - vt), :], ag_recv.at[0])
    first_pass(0, True)

    def first_step(g, carry):
        take(kv_s.at[pl.ds(0, chunk), :], ag_recv.at[g])
        first_pass(g, False)
        return carry

    lax.fori_loop(1, ng, first_step, 0)

    for g, j in pairs:
        to = peer(g, j)
        send(f_s.at[:, block(to, ds_cols)], fsl_s.at[mine, :], xs.at[0], xr.at[0], {"seq": to})
    fsl_s[mine, :] = f_s[:, block(me, ds_cols)]

    c_copy.wait()
    for h in range(heads):
        cols = pl.ds(h * hd, hd)
        both = ot_s[h].T
        inverse = 1.0 / both[:, hd:]
        context = both[:, :hd] * inverse
        ctx_s[:, cols] = context.astype(BF16)
        scaled = (c_s[:, cols].astype(F32) * inverse).astype(BF16)
        centre = -jnp.sum(context * scaled.astype(F32), axis=1, keepdims=True)
        high = centre.astype(BF16).astype(F32)
        low = centre - high
        extra = jnp.where(lane == 0, high, jnp.where(lane == 1, low, 0.0)).astype(BF16)
        rows = pl.ds(h * tokens, tokens)
        do_s[rows, pl.ds(0, hd)] = scaled
        do_s[rows, pl.ds(hd, hd)] = extra
    ctx_copy = pltpu.make_async_copy(ctx_s, ctx_hbm, out_sem.at[0])
    ctx_copy.start()

    def send_group(src, dst, send_sem, recv_sem, group, first):
        for j in range(first, GROUP_DEVICES):
            to = group * GROUP_DEVICES + lax.rem(my_place + j, GROUP_DEVICES)
            send(src.at[block(to, vt), :], dst.at[mine, :], send_sem, recv_sem, {"seq": to})

    def value_part(group):
        rows = block(group, chunk)
        sendv_s[rows, :] = dot(e_s[rows, :], do_s[:, pl.ds(0, hd)]).astype(BF16)

    def value_step(g, carry):
        group = lax.rem(my_group + g, ng)
        value_part(group)
        send_group(sendv_s, rsv_s, xs.at[1], xr.at[1], group, 0)
        return carry

    lax.fori_loop(1, ng, value_step, 0)
    value_part(my_group)
    send_group(sendv_s, rsv_s, xs.at[1], xr.at[1], my_group, 1)
    rsv_s[mine, :] = sendv_s[mine, :]

    lane_of_key = lax.broadcasted_iota(jnp.int32, (chunk, hd), 1)
    ones_two = jnp.where(lane_of_key < 2, 1.0, 0.0).astype(BF16)

    def key_part(group):
        rows = block(group, chunk)
        value_aug = jnp.concatenate([kv_s[rows, pl.ds(hd, hd)], ones_two], axis=1)
        for h in range(heads):
            head = pl.ds(h * tokens, tokens)
            part = dot_across(value_aug, do_s[head, :])
            e_s[rows, head] = (e_s[rows, head].astype(F32) * part).astype(BF16)
        sendk_s[rows, :] = (dot(e_s[rows, :], y_s[:, pl.ds(0, hd)]) * scale).astype(BF16)

    def key_step(g, carry):
        group = lax.rem(my_group + g, ng)
        key_part(group)
        send_group(sendk_s, rsk_s, xs.at[2], xr.at[2], group, 0)
        return carry

    lax.fori_loop(1, ng, key_step, 0)
    key_part(my_group)
    send_group(sendk_s, rsk_s, xs.at[2], xr.at[2], my_group, 1)
    rsk_s[mine, :] = sendk_s[mine, :]

    most = (ns - 1) * vt

    def add_up(ref):
        total = ref[pl.ds(0, vt), :].astype(F32)
        for s in range(1, ns):
            total = total + ref[pl.ds(s * vt, vt), :].astype(F32)
        return total

    take(rsv_s.at[pl.ds(0, most), :], xr.at[1])
    gv_s[mine, :] = add_up(rsv_s).astype(BF16)
    for g, j in pairs:
        send(gv_s.at[mine, :], gv_s.at[mine, :], xs.at[3], xr.at[3], {"seq": peer(g, j)})

    for h in range(heads):
        cols = pl.ds(h * hd, hd)
        upstream = dot(kt_s[...], e_s[:, pl.ds(h * tokens, tokens)]).T * scale
        qg_s[:, cols] = norm_back(q_s[:, cols].astype(F32), upstream).astype(BF16)
    qg_copy = pltpu.make_async_copy(qg_s, qg_hbm, out_sem.at[1])
    qg_copy.start()

    take(rsk_s.at[pl.ds(0, most), :], xr.at[2])
    gk_s[mine, :] = norm_back(key_s[...], add_up(rsk_s)).astype(BF16)
    for g, j in pairs:
        send(gk_s.at[mine, :], gk_s.at[mine, :], xs.at[4], xr.at[4], {"seq": peer(g, j)})

    row_grads = jnp.concatenate([gk_s[mine, :], gv_s[mine, :]], axis=1)
    for k in range(steps):
        rows = pl.ds(k * depth, depth)
        fg_s[:, rows] = dot_across(row_grads, w_s[rows, :]).astype(BF16)
    fg_copy = pltpu.make_async_copy(fg_s, fg_hbm, out_sem.at[2])
    fg_copy.start()

    take(fsl_s.at[pl.ds(0, most), :], xr.at[0])
    feats_t = fsl_s[...].astype(F32).T.astype(BF16)

    def reduce_first(part, grads):
        dp1_s[part] = dot(feats_t, grads[...]).astype(BF16)
        for o in range(1, nd):
            to = doc_peer(o)
            send(
                dp1_s.at[part, block(to, dp_rows), :],
                dp1r_s.at[part, block(doc, dp_rows), :],
                xs.at[5 + part],
                xr.at[5 + part],
                {"dp": to},
            )
        own = block(doc, dp_rows)
        dp1r_s[part, own, :] = dp1_s[part, own, :]

    def reduce_second(part):
        take(dp1r_s.at[part, pl.ds(0, (nd - 1) * dp_rows), :], xr.at[5 + part])
        total = dp1r_s[part, pl.ds(0, dp_rows), :].astype(F32)
        for s in range(1, nd):
            total = total + dp1r_s[part, pl.ds(s * dp_rows, dp_rows), :].astype(F32)
        own = block(doc, dp_rows)
        dp2_s[part, own, :] = total
        for o in range(1, nd):
            send(
                dp2_s.at[part, own, :],
                dp2_s.at[part, own, :],
                xs.at[7 + part],
                xr.at[7 + part],
                {"dp": doc_peer(o)},
            )

    take(gv_s.at[pl.ds(0, most), :], xr.at[3])
    reduce_first(0, gv_s)
    take(gk_s.at[pl.ds(0, most), :], xr.at[4])
    reduce_first(1, gk_s)
    reduce_second(0)
    reduce_second(1)
    out_copies = []
    for part, out in ((0, vw_hbm), (1, kw_hbm)):
        take(dp2_s.at[part, pl.ds(0, (nd - 1) * dp_rows), :], xr.at[7 + part])
        copy = pltpu.make_async_copy(dp2_s.at[part], out, out_sem.at[3 + part])
        copy.start()
        out_copies.append(copy)

    take(kv_s.at[pl.ds(0, most), :], ag_send.at[0])
    take(fsl_s.at[pl.ds(0, most), :], xs.at[0])
    for index, ref in ((1, sendv_s), (2, sendk_s), (3, gv_s), (4, gk_s)):
        take(ref.at[pl.ds(0, most), :], xs.at[index])
    for part in range(2):
        take(dp1_s.at[part, pl.ds(0, (nd - 1) * dp_rows), :], xs.at[5 + part])
        take(dp2_s.at[part, pl.ds(0, (nd - 1) * dp_rows), :], xs.at[7 + part])
    for copy in [ctx_copy, qg_copy, fg_copy] + out_copies:
        copy.wait()


def local(ns, nd, queries, image_feats, key_weight, value_weight, image_pos, image_slot, ctx_grad):
    d, hd = key_weight.shape
    tokens, width = queries.shape[1:]
    vt = image_feats.shape[2]
    heads = width // hd
    keys = ns * vt
    chunk = GROUP_DEVICES * vt
    ds_cols = d // ns
    dp_rows = ds_cols // nd
    rows = heads * tokens

    def lanes(row, fill):
        return jnp.pad(row, ((0, 0), (0, hd - row.shape[1])), constant_values=fill)

    anywhere = pl.BlockSpec(memory_space=pl.ANY)
    inside = pl.BlockSpec(memory_space=pltpu.VMEM)
    outs = pl.pallas_call(
        functools.partial(kernel, ns, nd),
        out_shape=(
            jax.ShapeDtypeStruct((tokens, width), BF16),
            jax.ShapeDtypeStruct((tokens, width), BF16),
            jax.ShapeDtypeStruct((vt, d), BF16),
            jax.ShapeDtypeStruct((ds_cols, hd), F32),
            jax.ShapeDtypeStruct((ds_cols, hd), F32),
        ),
        in_specs=[anywhere] * 4 + [inside] * 2 + [anywhere],
        out_specs=[anywhere] * 5,
        scratch_shapes=[
            pltpu.VMEM((tokens, width), BF16),
            pltpu.VMEM((tokens, width), BF16),
            pltpu.VMEM((vt, d), BF16),
            pltpu.VMEM((d, 2 * hd), BF16),
            pltpu.VMEM((vt, hd), F32),
            pltpu.VMEM((keys, 2 * hd), BF16),
            pltpu.VMEM((rows, 2 * hd), BF16),
            pltpu.VMEM((rows, 2 * hd), BF16),
            pltpu.VMEM((hd, keys), BF16),
            pltpu.VMEM((hd, keys), BF16),
            pltpu.VMEM((keys, rows), BF16),
            pltpu.VMEM((heads, 2 * hd, tokens), F32),
            pltpu.VMEM((tokens, width), BF16),
            pltpu.VMEM((tokens, width), BF16),
            pltpu.VMEM((vt, d), BF16),
            pltpu.VMEM((keys, ds_cols), BF16),
            pltpu.VMEM((keys, hd), BF16),
            pltpu.VMEM((keys, hd), BF16),
            pltpu.VMEM((keys, hd), BF16),
            pltpu.VMEM((keys, hd), BF16),
            pltpu.VMEM((keys, hd), BF16),
            pltpu.VMEM((keys, hd), BF16),
            pltpu.VMEM((2, ds_cols, hd), BF16),
            pltpu.VMEM((2, ds_cols, hd), BF16),
            pltpu.VMEM((2, ds_cols, hd), F32),
            pltpu.SemaphoreType.DMA((14,)),
            pltpu.SemaphoreType.DMA((5,)),
            pltpu.SemaphoreType.DMA((1,)),
            pltpu.SemaphoreType.DMA((ns // GROUP_DEVICES,)),
            pltpu.SemaphoreType.DMA((9,)),
            pltpu.SemaphoreType.DMA((9,)),
        ],
        compiler_params=pltpu.CompilerParams(
            collective_id=0, has_side_effects=True, vmem_limit_bytes=56 * 1024 * 1024
        ),
    )(
        queries[0],
        image_feats.reshape(vt, d),
        key_weight,
        value_weight,
        lanes(image_pos, 0),
        lanes(image_slot, -1),
        ctx_grad[0],
    )
    context, query_grad, feats_grad, key_wgrad, value_wgrad = outs
    return (
        context[None],
        query_grad[None],
        feats_grad.reshape(1, 1, vt, d),
        key_wgrad,
        value_wgrad,
    )


def solution(mesh):
    return jax.shard_map(
        functools.partial(local, mesh.shape["seq"], mesh.shape["dp"]),
        mesh=mesh,
        in_specs=(
            P("dp", "seq", None),
            P("dp", "seq", None, None),
            P(),
            P(),
            P("dp", None),
            P("dp", None),
            P("dp", "seq", None),
        ),
        out_specs=(
            P("dp", "seq", None),
            P("dp", "seq", None),
            P("dp", "seq", None, None),
            P("seq", None),
            P("seq", None),
        ),
        check_vma=False,
    )
```

time: 711 us -> 90.3 us (0.13)
  waiting for transfers between devices: 560 us -> 0 us
  matrix products: 82.4 us -> 0 us
  Pallas kernels: 0 us -> 81 us
  local copies, waits for them, and re-layouts: 37 us -> 8.47 us
  other arithmetic: 14.9 us -> 0 us
  between operations: 14 us -> 0.67 us
    reduce_scatter x2 -> x0, waiting for transfers between devices: 349 us -> none  [the longest x1 183 us: local(): lax.psum_scatter(lax.dot_general(feat_rows, row_grads, stacked, preferred...]
    all_gather x1 -> x0, waiting for transfers between devices: 127 us -> none  [local(): gathered = lax.all_gather(packed, 'seq', axis=0, tiled=True)]
    psum x1 -> x0, waiting for transfers between devices: 83.7 us -> none  [local(): wgrad_total = lax.psum(wgrad_piece, 'dp')]
    dot_general x29 -> x0, matrix products: 82.4 us -> none  [the longest x4 20.6 us: attend_block(): lax.dot_general(score_full, query_block.astype(jnp.float32), stacked, pre...]
    pallas_call x0 -> x1, Pallas kernels: none -> 81 us  [local(): pl.pallas_call(functools.partial(kernel, ns, nd), out_shape=(jax.ShapeDty...]
    while x72 -> x0, local copies, waits for them, and re-layouts: 12.7 us -> none
    mul x4 -> x0, local copies, waits for them, and re-layouts: 7.38 us -> none  [the longest x2 3.73 us: norm_back(): normed * jnp.mean(upstream * normed, axis=-1, keepdims=True)]
  transfers between devices with their start and end apart: 4 -> 0, of which waited for: 4 -> 0; matrix products, arithmetic and copies ran while one was open for 5% -> 0% of each run, Pallas kernels for 0% -> 0%
where the time goes in v1:
time: 90.3 us; the launch traced here: 90.2 us
  Pallas kernels  81 us (90%)
  local copies, waits for them, and re-layouts  8.47 us (9%)
    pallas_call x1, Pallas kernels, local(): pl.pallas_call(functools.partial(kernel, ns, nd), out_shape=(jax.ShapeDty...  81 us
    unnamed x11, local copies, waits for them, and re-layouts  6.13 us
    pad x2, local copies, waits for them, and re-layouts, lanes(): return jnp.pad(row, ((0, 0), (0, hd - row.shape[1])), constant_values=fill)  2.34 us

profile of v1, /device:TPU:1, one launch (start us, length us, event | category | flops | bytes accessed | tf_op | source)
XLA Modules:
  0.0 90.2 jit_solution(5713805725143753710)
XLA Ops:
  0.6 1.2 %pad.7.pos_ref = s32[1,128]{1,0:T(1,128)} pad(s32[1,32]{1,0:T(1,128)} %param.11, s32[]{:T(128)} %constant.0.clone.1), padding=0_0x0_96 | pad | bytes 644 | tf_op jit(solution)/shard_map/jit(_pad)/pad | solution.py:382
  1.8 1.2 %pad.8.slot_ref = s32[1,128]{1,0:T(1,128)} pad(s32[1,32]{1,0:T(1,128)} %param.12, s32[]{:T(128)} %constant.1.clone.1), padding=0_0x0_96 | pad | bytes 644 | tf_op jit(solution)/shard_map/jit(_pad)/pad | solution.py:382
  3.0 81.0 %shard_map.110 = (bf16[256,1024]{1,0:T(8,128)(2,1)}, bf16[256,1024]{1,0:T(8,128)(2,1)}, bf16[64,8192]{1,0:T(8,128)(2,1)}, f32[256,128]{1,0:T(8,128)}, f32[256,128]{1,0:T(8,128)}) custom-call(bf16[256,1024]{1,0:T(8,128)(2,1)} %bitcast.10, bf16[64,8192]{1,0:T(8,128)(2,1)} %bitcast.7, bf16[8192,128]{1,0:T(8,128)(2,1)} %wk_hbm.1, bf16[8192,128]{1,0:T(8,128)(2,1)} %wv_hbm.1, ...), custom_call_target="tpu_custom_call" | custom-call | tf_op jit(solution)/shard_map/pallas_call | solution.py:386
  84.0 0.0 copy-start
  84.0 0.0 copy-start.2
  84.0 0.0 copy-start.1
  84.0 2.0 %copy.17 = bf16[1,256,1024]{2,1,0:T(8,128)(2,1)} copy(bf16[1,256,1024]{2,1,0:T(8,128)(2,1)} %bitcast.9) | data formatting | bytes 1048576
  86.0 1.9 %copy.18 = bf16[1,256,1024]{2,1,0:T(8,128)(2,1)} copy(bf16[1,256,1024]{2,1,0:T(8,128)(2,1)} %bitcast.8) | data formatting | bytes 1048576
  87.9 0.0 copy-done
  87.9 1.0 %copy.19 = bf16[1,1,64,8192]{3,2,1,0:T(8,128)(2,1)} copy(bf16[1,1,64,8192]{3,2,1,0:T(8,128)(2,1)S(1)} %bitcast.6) | data formatting | bytes 2097152
  88.8 0.0 copy-done.2
  88.8 0.7 copy.20
  89.5 0.0 copy-done.1
  89.5 0.7 copy.21
Async XLA Ops:
  84.0 3.9 %copy-start = (bf16[64,8192]{1,0:T(8,128)(2,1)S(1)}, bf16[64,8192]{1,0:T(8,128)(2,1)}, u32[]{:S(2)}) copy-start(bf16[64,8192]{1,0:T(8,128)(2,1)} %get-tuple-element.12) | copy-start | bytes 3145732
  84.0 4.8 %copy-start.2 = (f32[256,128]{1,0:T(8,128)S(1)}, f32[256,128]{1,0:T(8,128)}, u32[]{:S(2)}) copy-start(f32[256,128]{1,0:T(8,128)} %get-tuple-element.23) | copy-start | bytes 393220
  84.0 5.5 %copy-start.1 = (f32[256,128]{1,0:T(8,128)S(1)}, f32[256,128]{1,0:T(8,128)}, u32[]{:S(2)}) copy-start(f32[256,128]{1,0:T(8,128)} %get-tuple-element.24) | copy-start | bytes 393220

commit v2 on v1

--- a/solution.py
+++ b/solution.py
@@ -11,6 +11,9 @@
 LOG2E = 1.4426950408889634
 HIDE = -30000.0
 GROUP_DEVICES = 4
+SPAN = 8
+EARLY, LATER, CUT = 28, 28, 5
+KV, FEATS, VSUM, KSUM, VALL, KALL, SUM1, SUM2, BOTH = 0, 1, 2, 3, 4, 5, 6, 8, 10
 BF16 = jnp.bfloat16
 F32 = jnp.float32
 MESH = pl.DeviceIdType.MESH
@@ -75,9 +78,9 @@
     dp1_s,
     dp1r_s,
     dp2_s,
+    wg_s,
     in_sem,
     out_sem,
-    ag_send,
     ag_recv,
     xs,
     xr,
@@ -91,18 +94,29 @@
     ng = ns // GROUP_DEVICES
     keys = ns * vt
     scale = hd ** (-0.5)
-    dp_rows = ds_cols // nd
+    half = ds_cols // 2
+    nx = ns // SPAN
+    nz = nd // 2
 
     me = lax.axis_index("seq")
     doc = lax.axis_index("dp")
     my_group = lax.div(me, GROUP_DEVICES)
     my_place = lax.rem(me, GROUP_DEVICES)
+    my_x = lax.div(me, SPAN)
+    my_r = lax.rem(me, SPAN)
+    my_zone = lax.div(doc, 2)
+    my_core = lax.rem(doc, 2)
 
     def peer(g, j):
         return lax.rem(my_group + g, ng) * GROUP_DEVICES + lax.rem(my_place + j, GROUP_DEVICES)
 
-    def doc_peer(o):
-        return lax.rem(doc + o, nd)
+    def span_peer(j):
+        return lax.rem(my_r + j, SPAN)
+
+    def zone_peer(o):
+        return {"dp": lax.rem(my_zone + o, nz) * 2 + my_core}
+
+    other_core = {"dp": my_zone * 2 + 1 - my_core}
 
     def block(index, size):
         return pl.ds(pl.multiple_of(index * size, size), size)
@@ -134,10 +148,55 @@
     c_copy.start()
 
     barrier = pltpu.get_barrier_semaphore()
-    for g, j in pairs:
-        pl.semaphore_signal(barrier, inc=1, device_id={"seq": peer(g, j)}, device_id_type=MESH)
-    for o in range(1, nd):
-        pl.semaphore_signal(barrier, inc=1, device_id={"dp": doc_peer(o)}, device_id_type=MESH)
+    lines = [(i, k) for i in range(nx) for k in range(2) if (i, k) != (0, 0)]
+    columns = [(j, x) for j in range(1, SPAN) for x in range(nx)]
+
+    def line_peer(i, k):
+        return lax.rem(my_x + i, nx), lax.rem(my_core + k, 2)
+
+    def line_device(i, k):
+        x, core = line_peer(i, k)
+        return {"dp": my_zone * 2 + core, "seq": x * SPAN + my_r}
+
+    def greet(device):
+        pl.semaphore_signal(barrier, inc=1, device_id=device, device_id_type=MESH)
+
+    for o in range(1, nz):
+        greet(zone_peer(o))
+    for i, k in lines:
+        if k:
+            greet(line_device(i, k))
+    for g, j in reversed(pairs):
+        greet({"seq": peer(g, j)})
+    greeted = ns - 1 + nx + nz - 1
+
+    mine = block(me, vt)
+
+    def send(phase, src, dst, target, arrival=None):
+        pltpu.make_async_remote_copy(
+            src_ref=src,
+            dst_ref=dst,
+            send_sem=xs.at[phase],
+            recv_sem=xr.at[phase] if arrival is None else arrival,
+            device_id=target,
+            device_id_type=MESH,
+        ).start()
+
+    def take(phase, ref, arrival=None):
+        pltpu.make_async_copy(ref, ref, xr.at[phase] if arrival is None else arrival).wait()
+
+    def sent(phase, ref):
+        pltpu.make_async_copy(ref, ref, xs.at[phase]).wait()
+
+    def send_feats(some):
+        for j, x in some:
+            to = span_peer(j)
+            send(
+                FEATS,
+                f_hbm.at[:, block(x * SPAN + to, ds_cols)],
+                fsl_s.at[block(my_r, vt), pl.ds(x * ds_cols, ds_cols)],
+                {"seq": my_x * SPAN + to},
+            )
 
     rows_kv = jnp.zeros((vt, 2 * hd), F32)
     for k in range(steps):
@@ -147,37 +206,29 @@
         rows_kv = rows_kv + dot(f_s[:, rows], w_s[rows, :])
     key_rows = rows_kv[:, :hd]
     key_s[...] = key_rows
-    mine = block(me, vt)
     kv_s[mine, :] = jnp.concatenate(
         [(key_rows * row_factor(key_rows)).astype(BF16), rows_kv[:, hd:].astype(BF16)], axis=1
     )
-    pl.semaphore_wait(barrier, ns - 1 + nd - 1)
-
-    def send(src, dst, send_sem, recv_sem, target):
-        pltpu.make_async_remote_copy(
-            src_ref=src,
-            dst_ref=dst,
-            send_sem=send_sem,
-            recv_sem=recv_sem,
-            device_id=target,
-            device_id_type=MESH,
-        ).start()
-
-    def take(ref, sem):
-        pltpu.make_async_copy(ref, ref, sem).wait()
-
-    for g, j in pairs:
-        send(kv_s.at[mine, :], kv_s.at[mine, :], ag_send.at[0], ag_recv.at[g], {"seq": peer(g, j)})
-
     lane = lax.broadcasted_iota(jnp.int32, (tokens, hd), 1)
     tok = me * tokens + lax.broadcasted_iota(jnp.int32, (tokens, hd), 0)
-    hidden = jnp.where(pos_ref[...] > tok, HIDE, 0.0).astype(BF16)
+    rest = hd - pos_ref.shape[1]
+    positions = jnp.concatenate([pos_ref[...], jnp.zeros((1, rest), jnp.int32)], axis=1)
+    slots = jnp.concatenate([slot_ref[...], jnp.full((1, rest), -1, jnp.int32)], axis=1)
+    hidden = jnp.where(positions > tok, HIDE, 0.0).astype(BF16)
     q_copy.wait()
     for h in range(heads):
         raw = q_s[:, pl.ds(h * hd, hd)].astype(F32)
         rows = pl.ds(h * tokens, tokens)
         y_s[rows, pl.ds(0, hd)] = (raw * row_factor(raw)).astype(BF16)
         y_s[rows, pl.ds(hd, hd)] = hidden
+
+    pl.semaphore_wait(barrier, greeted)
+    for g, j in pairs:
+        send(KV, kv_s.at[mine, :], kv_s.at[mine, :], {"seq": peer(g, j)}, ag_recv.at[g])
+    send_feats(columns[:EARLY])
+    for x in range(nx):
+        cols = block(x * SPAN + my_r, ds_cols)
+        fsl_s[block(my_r, vt), pl.ds(x * ds_cols, ds_cols)] = f_s[:, cols]
 
     def first_pass(g, first):
         group = lax.rem(my_group - g + ng, ng)
@@ -186,7 +237,7 @@
         slot_of_key = group * GROUP_DEVICES + lax.div(
             lax.broadcasted_iota(jnp.int32, (chunk, hd), 0), vt
         )
-        marks = (slot_ref[...] == slot_of_key).astype(F32).astype(BF16)
+        marks = (slots == slot_of_key).astype(F32).astype(BF16)
         key_aug = jnp.concatenate([pair[:, :hd], marks], axis=1)
         value_t = pair[:, hd:].astype(F32).T.astype(BF16)
         kt_s[:, rows] = pair[:, :hd].astype(F32).T.astype(BF16)
@@ -202,20 +253,17 @@
             else:
                 ot_s[h] += part
 
-    take(kv_s.at[pl.ds(0, chunk - vt), :], ag_recv.at[0])
+    take(KV, kv_s.at[pl.ds(0, chunk - vt), :], ag_recv.at[0])
     first_pass(0, True)
 
     def first_step(g, carry):
-        take(kv_s.at[pl.ds(0, chunk), :], ag_recv.at[g])
+        take(KV, kv_s.at[pl.ds(0, chunk), :], ag_recv.at[g])
         first_pass(g, False)
         return carry
 
     lax.fori_loop(1, ng, first_step, 0)
 
-    for g, j in pairs:
-        to = peer(g, j)
-        send(f_s.at[:, block(to, ds_cols)], fsl_s.at[mine, :], xs.at[0], xr.at[0], {"seq": to})
-    fsl_s[mine, :] = f_s[:, block(me, ds_cols)]
+    send_feats(columns[EARLY:LATER])
 
     c_copy.wait()
     for h in range(heads):
@@ -235,10 +283,10 @@
     ctx_copy = pltpu.make_async_copy(ctx_s, ctx_hbm, out_sem.at[0])
     ctx_copy.start()
 
-    def send_group(src, dst, send_sem, recv_sem, group, first):
+    def send_group(phase, src, dst, group, first):
         for j in range(first, GROUP_DEVICES):
             to = group * GROUP_DEVICES + lax.rem(my_place + j, GROUP_DEVICES)
-            send(src.at[block(to, vt), :], dst.at[mine, :], send_sem, recv_sem, {"seq": to})
+            send(phase, src.at[block(to, vt), :], dst.at[mine, :], {"seq": to})
 
     def value_part(group):
         rows = block(group, chunk)
@@ -247,12 +295,12 @@
     def value_step(g, carry):
         group = lax.rem(my_group + g, ng)
         value_part(group)
-        send_group(sendv_s, rsv_s, xs.at[1], xr.at[1], group, 0)
+        send_group(VSUM, sendv_s, rsv_s, group, 0)
         return carry
 
     lax.fori_loop(1, ng, value_step, 0)
     value_part(my_group)
-    send_group(sendv_s, rsv_s, xs.at[1], xr.at[1], my_group, 1)
+    send_group(VSUM, sendv_s, rsv_s, my_group, 1)
     rsv_s[mine, :] = sendv_s[mine, :]
 
     lane_of_key = lax.broadcasted_iota(jnp.int32, (chunk, hd), 1)
@@ -270,26 +318,34 @@
     def key_step(g, carry):
         group = lax.rem(my_group + g, ng)
         key_part(group)
-        send_group(sendk_s, rsk_s, xs.at[2], xr.at[2], group, 0)
+        send_group(KSUM, sendk_s, rsk_s, group, 0)
         return carry
 
-    lax.fori_loop(1, ng, key_step, 0)
+    def add_up(ref, size):
+        total = ref[pl.ds(0, size), :].astype(F32)
+        for s in range(1, ref.shape[0] // size):
+            total = total + ref[pl.ds(s * size, size), :].astype(F32)
+        return total
+
+    most = (ns - 1) * vt
+    span_most = (SPAN - 1) * vt
+    own = block(my_r, vt)
+
+    def send_all(phase, ref):
+        for j in range(1, SPAN):
+            send(phase, ref.at[own, :], ref.at[own, :], {"seq": my_x * SPAN + span_peer(j)})
+
+    lax.fori_loop(1, CUT, key_step, 0)
+
+    take(VSUM, rsv_s.at[pl.ds(0, most), :])
+    gv_s[own, :] = add_up(rsv_s, vt).astype(BF16)
+    send_all(VALL, gv_s)
+
+    lax.fori_loop(CUT, ng, key_step, 0)
     key_part(my_group)
-    send_group(sendk_s, rsk_s, xs.at[2], xr.at[2], my_group, 1)
+    send_group(KSUM, sendk_s, rsk_s, my_group, 1)
     rsk_s[mine, :] = sendk_s[mine, :]
-
-    most = (ns - 1) * vt
-
-    def add_up(ref):
-        total = ref[pl.ds(0, vt), :].astype(F32)
-        for s in range(1, ns):
-            total = total + ref[pl.ds(s * vt, vt), :].astype(F32)
-        return total
-
-    take(rsv_s.at[pl.ds(0, most), :], xr.at[1])
-    gv_s[mine, :] = add_up(rsv_s).astype(BF16)
-    for g, j in pairs:
-        send(gv_s.at[mine, :], gv_s.at[mine, :], xs.at[3], xr.at[3], {"seq": peer(g, j)})
+    send_feats(columns[LATER:])
 
     for h in range(heads):
         cols = pl.ds(h * hd, hd)
@@ -298,72 +354,91 @@
     qg_copy = pltpu.make_async_copy(qg_s, qg_hbm, out_sem.at[1])
     qg_copy.start()
 
-    take(rsk_s.at[pl.ds(0, most), :], xr.at[2])
-    gk_s[mine, :] = norm_back(key_s[...], add_up(rsk_s)).astype(BF16)
-    for g, j in pairs:
-        send(gk_s.at[mine, :], gk_s.at[mine, :], xs.at[4], xr.at[4], {"seq": peer(g, j)})
-
-    row_grads = jnp.concatenate([gk_s[mine, :], gv_s[mine, :]], axis=1)
+    def sum_first(part, grads):
+        dp1_s[part] = dot(feats_t, grads[...]).astype(BF16)
+        for i, k in lines:
+            x, core = line_peer(i, k)
+            send(
+                SUM1 + part,
+                dp1_s.at[part, block(x * 2 + core, half), :],
+                dp1r_s.at[part, block(my_x * 2 + my_core, half), :],
+                line_device(i, k),
+            )
+        slot = block(my_x * 2 + my_core, half)
+        dp1r_s[part, slot, :] = dp1_s[part, slot, :]
+
+    def sum_second(part):
+        take(SUM1 + part, dp1r_s.at[part, pl.ds(0, len(lines) * half), :])
+        slot = block(my_zone, half)
+        dp2_s[part, slot, :] = add_up(dp1r_s.at[part], half).astype(BF16)
+        for o in range(1, nz):
+            send(SUM2 + part, dp2_s.at[part, slot, :], dp2_s.at[part, slot, :], zone_peer(o))
+
+    def sum_third(part):
+        if nz > 1:
+            take(SUM2 + part, dp2_s.at[part, pl.ds(0, (nz - 1) * half), :])
+        slot = block(my_core, half)
+        wg_s[part, slot, :] = add_up(dp2_s.at[part], half)
+        send(BOTH + part, wg_s.at[part, slot, :], wg_s.at[part, slot, :], other_core)
+
+    def sum_last(part, out):
+        take(BOTH + part, wg_s.at[part, pl.ds(0, half), :])
+        copy = pltpu.make_async_copy(wg_s.at[part], out, out_sem.at[3 + part])
+        copy.start()
+        return copy
+
+    take(FEATS, fsl_s.at[pl.ds(0, span_most), :])
+    feats_t = fsl_s[...].astype(F32).T.astype(BF16)
+    take(VALL, gv_s.at[pl.ds(0, span_most), :])
+    sum_first(0, gv_s)
+
+    take(KSUM, rsk_s.at[pl.ds(0, most), :])
+    gk_s[own, :] = norm_back(key_s[...], add_up(rsk_s, vt)).astype(BF16)
+    send_all(KALL, gk_s)
+
+    row_grads = jnp.concatenate([gk_s[own, :], gv_s[own, :]], axis=1)
     for k in range(steps):
         rows = pl.ds(k * depth, depth)
         fg_s[:, rows] = dot_across(row_grads, w_s[rows, :]).astype(BF16)
     fg_copy = pltpu.make_async_copy(fg_s, fg_hbm, out_sem.at[2])
     fg_copy.start()
 
-    take(fsl_s.at[pl.ds(0, most), :], xr.at[0])
-    feats_t = fsl_s[...].astype(F32).T.astype(BF16)
-
-    def reduce_first(part, grads):
-        dp1_s[part] = dot(feats_t, grads[...]).astype(BF16)
-        for o in range(1, nd):
-            to = doc_peer(o)
-            send(
-                dp1_s.at[part, block(to, dp_rows), :],
-                dp1r_s.at[part, block(doc, dp_rows), :],
-                xs.at[5 + part],
-                xr.at[5 + part],
-                {"dp": to},
-            )
-        own = block(doc, dp_rows)
-        dp1r_s[part, own, :] = dp1_s[part, own, :]
-
-    def reduce_second(part):
-        take(dp1r_s.at[part, pl.ds(0, (nd - 1) * dp_rows), :], xr.at[5 + part])
-        total = dp1r_s[part, pl.ds(0, dp_rows), :].astype(F32)
-        for s in range(1, nd):
-            total = total + dp1r_s[part, pl.ds(s * dp_rows, dp_rows), :].astype(F32)
-        own = block(doc, dp_rows)
-        dp2_s[part, own, :] = total
-        for o in range(1, nd):
-            send(
-                dp2_s.at[part, own, :],
-                dp2_s.at[part, own, :],
-                xs.at[7 + part],
-                xr.at[7 + part],
-                {"dp": doc_peer(o)},
-            )
-
-    take(gv_s.at[pl.ds(0, most), :], xr.at[3])
-    reduce_first(0, gv_s)
-    take(gk_s.at[pl.ds(0, most), :], xr.at[4])
-    reduce_first(1, gk_s)
-    reduce_second(0)
-    reduce_second(1)
-    out_copies = []
-    for part, out in ((0, vw_hbm), (1, kw_hbm)):
-        take(dp2_s.at[part, pl.ds(0, (nd - 1) * dp_rows), :], xr.at[7 + part])
-        copy = pltpu.make_async_copy(dp2_s.at[part], out, out_sem.at[3 + part])
+    sum_second(0)
+    take(KALL, gk_s.at[pl.ds(0, span_most), :])
+    sum_first(1, gk_s)
+    sum_third(0)
+    sum_second(1)
+    out_copies = [sum_last(0, vw_hbm)]
+    sum_third(1)
+    out_copies.append(sum_last(1, kw_hbm))
+
+    for phase, ref in ((KV, kv_s), (VSUM, sendv_s), (KSUM, sendk_s)):
+        sent(phase, ref.at[pl.ds(0, most), :])
+    for phase, ref in ((FEATS, fsl_s), (VALL, gv_s), (KALL, gk_s)):
+        sent(phase, ref.at[pl.ds(0, span_most), :])
+    for part in range(2):
+        sent(SUM1 + part, dp1_s.at[part, pl.ds(0, len(lines) * half), :])
+        if nz > 1:
+            sent(SUM2 + part, dp2_s.at[part, pl.ds(0, (nz - 1) * half), :])
+        sent(BOTH + part, wg_s.at[part, pl.ds(0, half), :])
+    for copy in [ctx_copy, qg_copy, fg_copy] + out_copies:
+        copy.wait()
+
+
+def hand_over(*refs):
+    count = len(refs) // 3
+    sems = refs[-1]
+    arrivals, departures = [], []
+    for i in range(count):
+        held = refs[2 * count + i]
+        arrivals.append(pltpu.make_async_copy(refs[i], held, sems.at[0, i]))
+        departures.append(pltpu.make_async_copy(held, refs[count + i], sems.at[1, i]))
+    for copy in arrivals:
         copy.start()
-        out_copies.append(copy)
-
-    take(kv_s.at[pl.ds(0, most), :], ag_send.at[0])
-    take(fsl_s.at[pl.ds(0, most), :], xs.at[0])
-    for index, ref in ((1, sendv_s), (2, sendk_s), (3, gv_s), (4, gk_s)):
-        take(ref.at[pl.ds(0, most), :], xs.at[index])
-    for part in range(2):
-        take(dp1_s.at[part, pl.ds(0, (nd - 1) * dp_rows), :], xs.at[5 + part])
-        take(dp2_s.at[part, pl.ds(0, (nd - 1) * dp_rows), :], xs.at[7 + part])
-    for copy in [ctx_copy, qg_copy, fg_copy] + out_copies:
+    for arrival, departure in zip(arrivals, departures):
+        arrival.wait()
+        departure.start()
+    for copy in departures:
         copy.wait()
 
 
@@ -375,11 +450,8 @@
     keys = ns * vt
     chunk = GROUP_DEVICES * vt
     ds_cols = d // ns
-    dp_rows = ds_cols // nd
+    nx = ns // SPAN
     rows = heads * tokens
-
-    def lanes(row, fill):
-        return jnp.pad(row, ((0, 0), (0, hd - row.shape[1])), constant_values=fill)
 
     anywhere = pl.BlockSpec(memory_space=pl.ANY)
     inside = pl.BlockSpec(memory_space=pltpu.VMEM)
@@ -410,22 +482,22 @@
             pltpu.VMEM((tokens, width), BF16),
             pltpu.VMEM((tokens, width), BF16),
             pltpu.VMEM((vt, d), BF16),
-            pltpu.VMEM((keys, ds_cols), BF16),
+            pltpu.VMEM((SPAN * vt, nx * ds_cols), BF16),
             pltpu.VMEM((keys, hd), BF16),
             pltpu.VMEM((keys, hd), BF16),
             pltpu.VMEM((keys, hd), BF16),
             pltpu.VMEM((keys, hd), BF16),
-            pltpu.VMEM((keys, hd), BF16),
-            pltpu.VMEM((keys, hd), BF16),
-            pltpu.VMEM((2, ds_cols, hd), BF16),
-            pltpu.VMEM((2, ds_cols, hd), BF16),
+            pltpu.VMEM((SPAN * vt, hd), BF16),
+            pltpu.VMEM((SPAN * vt, hd), BF16),
+            pltpu.VMEM((2, nx * ds_cols, hd), BF16),
+            pltpu.VMEM((2, nx * ds_cols, hd), BF16),
+            pltpu.VMEM((2, nd // 2 * ds_cols // 2, hd), BF16),
             pltpu.VMEM((2, ds_cols, hd), F32),
             pltpu.SemaphoreType.DMA((14,)),
             pltpu.SemaphoreType.DMA((5,)),
-            pltpu.SemaphoreType.DMA((1,)),
             pltpu.SemaphoreType.DMA((ns // GROUP_DEVICES,)),
-            pltpu.SemaphoreType.DMA((9,)),
-            pltpu.SemaphoreType.DMA((9,)),
+            pltpu.SemaphoreType.DMA((12,)),
+            pltpu.SemaphoreType.DMA((12,)),
         ],
         compiler_params=pltpu.CompilerParams(
             collective_id=0, has_side_effects=True, vmem_limit_bytes=56 * 1024 * 1024
@@ -435,11 +507,19 @@
         image_feats.reshape(vt, d),
         key_weight,
         value_weight,
-        lanes(image_pos, 0),
-        lanes(image_slot, -1),
+        image_pos,
+        image_slot,
         ctx_grad[0],
     )
-    context, query_grad, feats_grad, key_wgrad, value_wgrad = outs
+    context, query_grad, feats_grad, key_wgrad, value_wgrad = pl.pallas_call(
+        hand_over,
+        out_shape=tuple(jax.ShapeDtypeStruct(out.shape, out.dtype) for out in outs),
+        in_specs=[anywhere] * 5,
+        out_specs=[anywhere] * 5,
+        scratch_shapes=[pltpu.VMEM(out.shape, out.dtype) for out in outs]
+        + [pltpu.SemaphoreType.DMA((2, 5))],
+        compiler_params=pltpu.CompilerParams(vmem_limit_bytes=60 * 1024 * 1024),
+    )(*outs)
     return (
         context[None],
         query_grad[None],

time: 90.3 us -> 74.8 us (0.83)
  local copies, waits for them, and re-layouts: 8.47 us -> 0 us
  Pallas kernels: 81 us -> 74 us
    pallas_call x1, Pallas kernels: 81 us -> 71.3 us  [local(): pl.pallas_call(functools.partial(kernel, ns, nd), out_shape=(jax.ShapeDty...]
    unnamed x11 -> x0, local copies, waits for them, and re-layouts: 6.13 us -> none
    pallas_call x0 -> x1, Pallas kernels: none -> 2.68 us  [local(): pl.pallas_call(hand_over, out_shape=tuple((jax.ShapeDtypeStruct(out.shape...]
    pad x2 -> x0, local copies, waits for them, and re-layouts: 2.34 us -> none  [lanes(): return jnp.pad(row, ((0, 0), (0, hd - row.shape[1])), constant_values=fill)]
where the time goes in v2:
time: 74.8 us; the launch traced here: 74.6 us
  Pallas kernels  74 us (99%)
    pallas_call x1, Pallas kernels, local(): pl.pallas_call(functools.partial(kernel, ns, nd), out_shape=(jax.ShapeDty...  71.3 us
    pallas_call x1, Pallas kernels, local(): pl.pallas_call(hand_over, out_shape=tuple((jax.ShapeDtypeStruct(out.shape...  2.68 us

profile of v2, /device:TPU:1, one launch (start us, length us, event | category | flops | bytes accessed | tf_op | source)
XLA Modules:
  0.0 74.6 jit_solution(10156308131712109311)
XLA Ops:
  0.6 71.3 %shard_map.110 = (bf16[256,1024]{1,0:T(8,128)(2,1)}, bf16[256,1024]{1,0:T(8,128)(2,1)}, bf16[64,8192]{1,0:T(8,128)(2,1)}, f32[256,128]{1,0:T(8,128)}, f32[256,128]{1,0:T(8,128)}) custom-call(bf16[256,1024]{1,0:T(8,128)(2,1)} %bitcast.7, bf16[64,8192]{1,0:T(8,128)(2,1)} %bitcast.6, bf16[8192,128]{1,0:T(8,128)(2,1)} %wk_hbm.1, bf16[8192,128]{1,0:T(8,128)(2,1)} %wv_hbm.1, ...), custom_call_target="tpu_custom_call" | custom-call | tf_op jit(solution)/shard_map/pallas_call | solution.py:458
  72.0 2.7 %shard_map.111 = (bf16[256,1024]{1,0:T(8,128)(2,1)}, bf16[256,1024]{1,0:T(8,128)(2,1)}, bf16[64,8192]{1,0:T(8,128)(2,1)}, f32[256,128]{1,0:T(8,128)}, f32[256,128]{1,0:T(8,128)}) custom-call(bf16[256,1024]{1,0:T(8,128)(2,1)} %get-tuple-element.15.refs_0_, bf16[256,1024]{1,0:T(8,128)(2,1)} %get-tuple-element.16.refs_1_, ...), custom_call_target="tpu_custom_call" | custom-call | tf_op jit(solution)/shard_map/pallas_call | solution.py:514

commit v3 on v2

--- a/solution.py
+++ b/solution.py
@@ -12,7 +12,7 @@
 HIDE = -30000.0
 GROUP_DEVICES = 4
 SPAN = 8
-EARLY, LATER, CUT = 28, 28, 5
+PIECES = 1
 KV, FEATS, VSUM, KSUM, VALL, KALL, SUM1, SUM2, BOTH = 0, 1, 2, 3, 4, 5, 6, 8, 10
 BF16 = jnp.bfloat16
 F32 = jnp.float32
@@ -225,7 +225,7 @@
     pl.semaphore_wait(barrier, greeted)
     for g, j in pairs:
         send(KV, kv_s.at[mine, :], kv_s.at[mine, :], {"seq": peer(g, j)}, ag_recv.at[g])
-    send_feats(columns[:EARLY])
+    send_feats(columns)
     for x in range(nx):
         cols = block(x * SPAN + my_r, ds_cols)
         fsl_s[block(my_r, vt), pl.ds(x * ds_cols, ds_cols)] = f_s[:, cols]
@@ -263,7 +263,6 @@
 
     lax.fori_loop(1, ng, first_step, 0)
 
-    send_feats(columns[EARLY:LATER])
 
     c_copy.wait()
     for h in range(heads):
@@ -335,17 +334,14 @@
         for j in range(1, SPAN):
             send(phase, ref.at[own, :], ref.at[own, :], {"seq": my_x * SPAN + span_peer(j)})
 
-    lax.fori_loop(1, CUT, key_step, 0)
+    lax.fori_loop(1, ng, key_step, 0)
+    key_part(my_group)
+    send_group(KSUM, sendk_s, rsk_s, my_group, 1)
+    rsk_s[mine, :] = sendk_s[mine, :]
 
     take(VSUM, rsv_s.at[pl.ds(0, most), :])
     gv_s[own, :] = add_up(rsv_s, vt).astype(BF16)
     send_all(VALL, gv_s)
-
-    lax.fori_loop(CUT, ng, key_step, 0)
-    key_part(my_group)
-    send_group(KSUM, sendk_s, rsk_s, my_group, 1)
-    rsk_s[mine, :] = sendk_s[mine, :]
-    send_feats(columns[LATER:])
 
     for h in range(heads):
         cols = pl.ds(h * hd, hd)
@@ -387,14 +383,14 @@
         copy.start()
         return copy
 
+    take(KSUM, rsk_s.at[pl.ds(0, most), :])
+    gk_s[own, :] = norm_back(key_s[...], add_up(rsk_s, vt)).astype(BF16)
+    send_all(KALL, gk_s)
+
     take(FEATS, fsl_s.at[pl.ds(0, span_most), :])
     feats_t = fsl_s[...].astype(F32).T.astype(BF16)
     take(VALL, gv_s.at[pl.ds(0, span_most), :])
     sum_first(0, gv_s)
-
-    take(KSUM, rsk_s.at[pl.ds(0, most), :])
-    gk_s[own, :] = norm_back(key_s[...], add_up(rsk_s, vt)).astype(BF16)
-    send_all(KALL, gk_s)
 
     row_grads = jnp.concatenate([gk_s[own, :], gv_s[own, :]], axis=1)
     for k in range(steps):
@@ -403,14 +399,13 @@
     fg_copy = pltpu.make_async_copy(fg_s, fg_hbm, out_sem.at[2])
     fg_copy.start()
 
-    sum_second(0)
     take(KALL, gk_s.at[pl.ds(0, span_most), :])
     sum_first(1, gk_s)
+    sum_second(0)
+    sum_second(1)
     sum_third(0)
-    sum_second(1)
-    out_copies = [sum_last(0, vw_hbm)]
     sum_third(1)
-    out_copies.append(sum_last(1, kw_hbm))
+    out_copies = [sum_last(0, vw_hbm), sum_last(1, kw_hbm)]
 
     for phase, ref in ((KV, kv_s), (VSUM, sendv_s), (KSUM, sendk_s)):
         sent(phase, ref.at[pl.ds(0, most), :])
@@ -431,8 +426,14 @@
     arrivals, departures = [], []
     for i in range(count):
         held = refs[2 * count + i]
-        arrivals.append(pltpu.make_async_copy(refs[i], held, sems.at[0, i]))
-        departures.append(pltpu.make_async_copy(held, refs[count + i], sems.at[1, i]))
+        size = held.shape[0] // PIECES
+        for p in range(PIECES):
+            rows = pl.ds(p * size, size)
+            n = i * PIECES + p
+            arrivals.append(pltpu.make_async_copy(refs[i].at[rows, :], held.at[rows, :], sems.at[0, n]))
+            departures.append(
+                pltpu.make_async_copy(held.at[rows, :], refs[count + i].at[rows, :], sems.at[1, n])
+            )
     for copy in arrivals:
         copy.start()
     for arrival, departure in zip(arrivals, departures):
@@ -517,7 +518,7 @@
         in_specs=[anywhere] * 5,
         out_specs=[anywhere] * 5,
         scratch_shapes=[pltpu.VMEM(out.shape, out.dtype) for out in outs]
-        + [pltpu.SemaphoreType.DMA((2, 5))],
+        + [pltpu.SemaphoreType.DMA((2, 5 * PIECES))],
         compiler_params=pltpu.CompilerParams(vmem_limit_bytes=60 * 1024 * 1024),
     )(*outs)
     return (

time: 74.8 us -> 73.3 us (0.980)
  Pallas kernels: 74 us -> 72.5 us
    pallas_call x1, Pallas kernels: 71.3 us -> 69.8 us  [local(): pl.pallas_call(functools.partial(kernel, ns, nd), out_shape=(jax.ShapeDty...]
where the time goes in v3:
time: 73.3 us; the launch traced here: 73.2 us
  Pallas kernels  72.5 us (99%)
    pallas_call x1, Pallas kernels, local(): pl.pallas_call(functools.partial(kernel, ns, nd), out_shape=(jax.ShapeDty...  69.8 us
    pallas_call x1, Pallas kernels, local(): pl.pallas_call(hand_over, out_shape=tuple((jax.ShapeDtypeStruct(out.shape...  2.68 us

profile of v3, /device:TPU:1, one launch (start us, length us, event | category | flops | bytes accessed | tf_op | source)
XLA Modules:
  0.0 73.2 jit_solution(13062902090417404211)
XLA Ops:
  0.6 69.8 %shard_map.110 = (bf16[256,1024]{1,0:T(8,128)(2,1)}, bf16[256,1024]{1,0:T(8,128)(2,1)}, bf16[64,8192]{1,0:T(8,128)(2,1)}, f32[256,128]{1,0:T(8,128)}, f32[256,128]{1,0:T(8,128)}) custom-call(bf16[256,1024]{1,0:T(8,128)(2,1)} %bitcast.7, bf16[64,8192]{1,0:T(8,128)(2,1)} %bitcast.6, bf16[8192,128]{1,0:T(8,128)(2,1)} %wk_hbm.1, bf16[8192,128]{1,0:T(8,128)(2,1)} %wv_hbm.1, ...), custom_call_target="tpu_custom_call" | custom-call | tf_op jit(solution)/shard_map/pallas_call | solution.py:459
  70.5 2.7 %shard_map.111 = (bf16[256,1024]{1,0:T(8,128)(2,1)}, bf16[256,1024]{1,0:T(8,128)(2,1)}, bf16[64,8192]{1,0:T(8,128)(2,1)}, f32[256,128]{1,0:T(8,128)}, f32[256,128]{1,0:T(8,128)}) custom-call(bf16[256,1024]{1,0:T(8,128)(2,1)} %get-tuple-element.15.refs_0_, bf16[256,1024]{1,0:T(8,128)(2,1)} %get-tuple-element.16.refs_1_, ...), custom_call_target="tpu_custom_call" | custom-call | tf_op jit(solution)/shard_map/pallas_call | solution.py:515

commit v4 on v3

--- a/solution.py
+++ b/solution.py
@@ -339,10 +339,6 @@
     send_group(KSUM, sendk_s, rsk_s, my_group, 1)
     rsk_s[mine, :] = sendk_s[mine, :]
 
-    take(VSUM, rsv_s.at[pl.ds(0, most), :])
-    gv_s[own, :] = add_up(rsv_s, vt).astype(BF16)
-    send_all(VALL, gv_s)
-
     for h in range(heads):
         cols = pl.ds(h * hd, hd)
         upstream = dot(kt_s[...], e_s[:, pl.ds(h * tokens, tokens)]).T * scale
@@ -367,7 +363,7 @@
         take(SUM1 + part, dp1r_s.at[part, pl.ds(0, len(lines) * half), :])
         slot = block(my_zone, half)
         dp2_s[part, slot, :] = add_up(dp1r_s.at[part], half).astype(BF16)
-        for o in range(1, nz):
+        for o in sorted(range(1, nz), key=lambda o: -min(o, nz - o)):
             send(SUM2 + part, dp2_s.at[part, slot, :], dp2_s.at[part, slot, :], zone_peer(o))
 
     def sum_third(part):
@@ -383,12 +379,17 @@
         copy.start()
         return copy
 
+    take(VSUM, rsv_s.at[pl.ds(0, most), :])
+    gv_s[own, :] = add_up(rsv_s, vt).astype(BF16)
+    send_all(VALL, gv_s)
+
+    take(FEATS, fsl_s.at[pl.ds(0, span_most), :])
+    feats_t = fsl_s[...].astype(F32).T.astype(BF16)
+
     take(KSUM, rsk_s.at[pl.ds(0, most), :])
     gk_s[own, :] = norm_back(key_s[...], add_up(rsk_s, vt)).astype(BF16)
     send_all(KALL, gk_s)
 
-    take(FEATS, fsl_s.at[pl.ds(0, span_most), :])
-    feats_t = fsl_s[...].astype(F32).T.astype(BF16)
     take(VALL, gv_s.at[pl.ds(0, span_most), :])
     sum_first(0, gv_s)
 

time: 73.3 us -> 72.7 us (level)
  no operation moved by 1% of the time
where the time goes in v4:
time: 72.7 us; the launch traced here: 72.5 us
  Pallas kernels  71.9 us (99%)
    pallas_call x1, Pallas kernels, local(): pl.pallas_call(functools.partial(kernel, ns, nd), out_shape=(jax.ShapeDty...  69.2 us
    pallas_call x1, Pallas kernels, local(): pl.pallas_call(hand_over, out_shape=tuple((jax.ShapeDtypeStruct(out.shape...  2.68 us

profile of v4, /device:TPU:1, one launch (start us, length us, event | category | flops | bytes accessed | tf_op | source)
XLA Modules:
  0.0 72.5 jit_solution(6166866137886634769)
XLA Ops:
  0.6 69.2 %shard_map.110 = (bf16[256,1024]{1,0:T(8,128)(2,1)}, bf16[256,1024]{1,0:T(8,128)(2,1)}, bf16[64,8192]{1,0:T(8,128)(2,1)}, f32[256,128]{1,0:T(8,128)}, f32[256,128]{1,0:T(8,128)}) custom-call(bf16[256,1024]{1,0:T(8,128)(2,1)} %bitcast.7, bf16[64,8192]{1,0:T(8,128)(2,1)} %bitcast.6, bf16[8192,128]{1,0:T(8,128)(2,1)} %wk_hbm.1, bf16[8192,128]{1,0:T(8,128)(2,1)} %wv_hbm.1, ...), custom_call_target="tpu_custom_call" | custom-call | tf_op jit(solution)/shard_map/pallas_call | solution.py:460
  69.9 2.7 %shard_map.111 = (bf16[256,1024]{1,0:T(8,128)(2,1)}, bf16[256,1024]{1,0:T(8,128)(2,1)}, bf16[64,8192]{1,0:T(8,128)(2,1)}, f32[256,128]{1,0:T(8,128)}, f32[256,128]{1,0:T(8,128)}) custom-call(bf16[256,1024]{1,0:T(8,128)(2,1)} %get-tuple-element.15.refs_0_, bf16[256,1024]{1,0:T(8,128)(2,1)} %get-tuple-element.16.refs_1_, ...), custom_call_target="tpu_custom_call" | custom-call | tf_op jit(solution)/shard_map/pallas_call | solution.py:516
